TPU v7x, 512 devices: a whole 4x4x16 slice. The times are simulated.
512 devices in a mesh: tm: 32 (over z_lo, x, core), space: 16 (over z_hi, y).
Axes of the slice: x: 4, y: 4, z: 16 (z_hi: 4, z_lo: 4; z = z_hi * 4 + z_lo), core: 2. Of those that a mesh axis runs over, the one named last changes fastest.
Arguments:
- initial_state: float32 [768, 512], P('space'), may hold values from -6 to 6
- velocity: bfloat16 [768, 512], P('space'), may hold values from -0.5 to 0.5
- diffusion: bfloat16 [768, 512], P('space'), may hold values from 0.25 to 0.5
- forcing: bfloat16 [256, 768, 512], P('tm', 'space'), may hold values from -6 to 6
- implicit: float32 [512, 512], replicated, may hold values from 0 to 1
- coarse_implicit: float32 [512, 512], replicated, may hold values from 0 to 1
Outputs:
- solution: float32 [256, 768, 512], P('tm', 'space')
All inputs are finite; a program needn't handle non-finite values.
Results may differ from a plain program's by a relative error of at most 0.0003.
Values may be sent and summed in bfloat16 or wider, within the bound.
A program may use at most 64 MiB of HBM per device.

v0:
```python
import jax
import jax.numpy as jnp
from jax import lax
from jax.sharding import PartitionSpec as P

CYCLES = 2
HIGHEST = lax.Precision.HIGHEST


def with_halo(cells, sides, width):
    for axis, dim in sides:
        count = lax.axis_size(axis)
        head = lax.slice_in_dim(cells, 0, width, axis=dim)
        tail = lax.slice_in_dim(cells, cells.shape[dim] - width, cells.shape[dim], axis=dim)
        cells = jnp.concatenate(
            [
                lax.ppermute(tail, axis, [(i, (i + 1) % count) for i in range(count)]),
                cells,
                lax.ppermute(head, axis, [((i + 1) % count, i) for i in range(count)]),
            ],
            axis=dim,
        )
    return cells


def from_behind(block, axis, distance):
    devices = range(lax.axis_size(axis))
    route = [(i - distance, i) for i in devices if i - distance in devices]
    return lax.ppermute(block, axis, route)


def stencil_weights(velocity, diffusion):
    moving = velocity.astype(jnp.float32)
    spread = diffusion.astype(jnp.float32)
    return (spread + 0.5 * moving, 1.0 - 2.0 * spread, spread - 0.5 * moving)


def apply_matrix(field, matrix):
    return jnp.dot(field, matrix, precision=HIGHEST, preferred_element_type=jnp.float32)


def per_device(initial_state, velocity, diffusion, forcing, implicit, coarse_implicit):
    block_steps = forcing.shape[0]
    weights = stencil_weights(velocity, diffusion)
    first_block = lax.axis_index("tm") == 0

    def relax_block(begin_state, step_count):
        values = []
        current = begin_state
        for offset in range(step_count):
            padded = with_halo(current, (("space", 0),), 1)
            summed = (
                weights[1] * current
                + weights[2] * padded[2:]
                + weights[0] * padded[:-2]
                + forcing[offset].astype(jnp.float32)
            )
            current = apply_matrix(summed, implicit)
            values.append(current)
        return values

    def previous(end_values):
        arrived = from_behind(end_values, "tm", 1)
        return jnp.where(first_block, initial_state, arrived)

    end_values = jnp.zeros_like(initial_state)
    for repeat in range(CYCLES):
        if repeat == 0:
            begin_state = jnp.where(first_block, initial_state, jnp.zeros_like(initial_state))
        else:
            begin_state = previous(end_values)
        end_values = relax_block(begin_state, block_steps)[-1]
        residual = relax_block(previous(end_values), block_steps)[-1] - end_values
        gathered = lax.all_gather(
            residual[None].astype(jnp.bfloat16), "tm", axis=0, tiled=True
        ).astype(jnp.float32)

        def coarse_turn(source, carried):
            return apply_matrix(carried, coarse_implicit) + gathered[source]

        end_values = end_values + lax.fori_loop(
            1, lax.axis_index("tm") + 1, coarse_turn, gathered[0]
        )
    values = relax_block(previous(end_values), block_steps - 1)
    return jnp.stack(values + [end_values], axis=0)


def solution(mesh):
    in_specs = (
        P("space", None),
        P("space", None),
        P("space", None),
        P("tm", "space", None),
        P(),
        P(),
    )
    out_specs = P("tm", "space", None)
    return jax.shard_map(
        per_device, mesh=mesh, in_specs=in_specs, out_specs=out_specs, check_vma=False
    )
```

profile of v0, /device:TPU:102, one launch (start us, length us, event | category | flops | bytes accessed | tf_op | source)
XLA Modules:
  0.0 854.1 jit_solution(8484713304822959292)
XLA Ops:
  6.6 12.6 %collective-permute-start = (f32[1,512]{1,0:T(1,128)S(1)}, f32[1,512]{1,0:T(1,128)S(1)}, u32[]{:S(2)}, u32[]{:S(2)}) collective-permute-start(f32[1,512]{1,0:T(1,128)S(1)} %get-tuple-element.159), channel_id=1, source_target_pairs={{1,0},{2,1},{3,2},{4,3},{5,4},{6,5},{7,6},{8,7},{9,8},{10,9},{11,1... | collective-permute-start | bytes 6152 | tf_op jit(solution)/shard_map/ppermute | solution.py:19
  21.2 9.6 %collective-permute-done.1 = f32[1,512]{1,0:T(1,128)S(1)} collective-permute-done((f32[1,512]{1,0:T(1,128)S(1)}, f32[1,512]{1,0:T(1,128)S(1)}, u32[]{:S(2)}, u32[]{:S(2)}) %collective-permute-start.1) | collective-permute-done | bytes 2080 | tf_op jit(solution)/shard_map/ppermute | solution.py:17
  38.2 7.6 collective-permute-done.3
  53.3 7.6 collective-permute-done.5
  68.4 7.6 collective-permute-done.7
  83.6 7.6 collective-permute-done.9
  98.6 7.6 collective-permute-done.11
  113.6 7.6 collective-permute-done.13
  128.7 7.6 collective-permute-done.15
  149.6 7.6 collective-permute-done.18
  163.9 7.6 collective-permute-done.20
  178.1 7.6 collective-permute-done.22
  192.3 7.6 collective-permute-done.24
  206.6 7.6 collective-permute-done.26
  258.4 55.3 %all-gather.5.cloned.1.call-done = bf16[1536,512]{1,0:T(8,128)(2,1)} async-done(((bf16[48,512]{1,0:T(8,128)(2,1)}), bf16[1536,512]{1,0:T(8,128)(2,1)}) %all-gather.5.cloned.1.call-update) | async-done | bytes 1572880 | tf_op jit(solution)/shard_map/all_gather | solution.py:74
  318.1 50.1 %while.20 = (s32[]{:T(128)}, f32[48,512]{1,0:T(8,128)S(1)}, s32[]{:T(128)}, f32[512,512]{1,0:T(8,128)S(1)}, f32[32,48,512]{2,1,0:T(8,128)}, /*index=5*/s32[]{:T(128)}, s32[]{:T(128)}, s32[]{:T(128)}) while((s32[]{:T(128)}, f32[48,512]{1,0:T(8,128)S(1)}, s32[]{:T(128)}, f32[512,512]{1,0:T(8,128)S(1)}, f32[32,48,512]{2,1,0:T(8,128)}, ...), condition=%wide.region_1.2_spmd, body=%wide.region_0.1_spmd.sunk | while | flops 151019520 | bytes 1540219 | solution.py:81
  374.2 9.1 %collective-permute-start.34 = (f32[1,512]{1,0:T(1,128)S(1)}, f32[1,512]{1,0:T(1,128)S(1)}, u32[]{:S(2)}, u32[]{:S(2)}) collective-permute-start(f32[1,512]{1,0:T(1,128)S(1)} %get-tuple-element.127), channel_id=1, source_target_pairs={{1,0},{2,1},{3,2},{4,3},{5,4},{6,5},{7,6},{8,7},{9,8},{10,9},{11,1... | collective-permute-start | bytes 6152 | tf_op jit(solution)/shard_map/ppermute | solution.py:19
  385.2 9.6 %collective-permute-done.35 = f32[1,512]{1,0:T(1,128)S(1)} collective-permute-done((f32[1,512]{1,0:T(1,128)S(1)}, f32[1,512]{1,0:T(1,128)S(1)}, u32[]{:S(2)}, u32[]{:S(2)}) %collective-permute-start.35) | collective-permute-done | bytes 2080 | tf_op jit(solution)/shard_map/ppermute | solution.py:17
  613.0 7.6 collective-permute-done.66
  622.0 56.5 %all-gather.7.cloned.1.call-done = bf16[1536,512]{1,0:T(8,128)(2,1)} async-done(((bf16[48,512]{1,0:T(8,128)(2,1)}), bf16[1536,512]{1,0:T(8,128)(2,1)}) %all-gather.7.cloned.1.call-update) | async-done | bytes 1572880 | tf_op jit(solution)/shard_map/all_gather | solution.py:74
  682.8 50.1 %while.21 = (s32[]{:T(128)}, f32[48,512]{1,0:T(8,128)S(1)}, s32[]{:T(128)}, f32[512,512]{1,0:T(8,128)S(1)}, f32[32,48,512]{2,1,0:T(8,128)}, /*index=5*/s32[]{:T(128)}, s32[]{:T(128)}, s32[]{:T(128)}) while((s32[]{:T(128)}, f32[48,512]{1,0:T(8,128)S(1)}, s32[]{:T(128)}, f32[512,512]{1,0:T(8,128)S(1)}, f32[32,48,512]{2,1,0:T(8,128)}, ...), condition=%wide.region_3.4_spmd, body=%wide.region_2.3_spmd.sunk | while | flops 151019520 | bytes 1540219 | solution.py:81
  738.9 9.1 %collective-permute-start.68 = (f32[1,512]{1,0:T(1,128)S(1)}, f32[1,512]{1,0:T(1,128)S(1)}, u32[]{:S(2)}, u32[]{:S(2)}) collective-permute-start(f32[1,512]{1,0:T(1,128)S(1)} %get-tuple-element.95), channel_id=1, source_target_pairs={{1,0},{2,1},{3,2},{4,3},{5,4},{6,5},{7,6},{8,7},{9,8},{10,9},{11,1... | collective-permute-start | bytes 6152 | tf_op jit(solution)/shard_map/ppermute | solution.py:19
  750.0 9.6 %collective-permute-done.69 = f32[1,512]{1,0:T(1,128)S(1)} collective-permute-done((f32[1,512]{1,0:T(1,128)S(1)}, f32[1,512]{1,0:T(1,128)S(1)}, u32[]{:S(2)}, u32[]{:S(2)}) %collective-permute-start.69) | collective-permute-done | bytes 2080 | tf_op jit(solution)/shard_map/ppermute | solution.py:17
  780.4 7.6 collective-permute-done.73
  (372 shorter events, 559.6 us)
Async XLA Ops:
  6.5 307.2 %all-gather.5.cloned.1.call-start = ((), (), s32[]{:S(2)}) async-start(), calls=%async_computation | async-start | bytes 1622016 | tf_op jit(solution)/shard_map/all_gather | solution.py:74
  6.6 14.6 %collective-permute-start = (f32[1,512]{1,0:T(1,128)S(1)}, f32[1,512]{1,0:T(1,128)S(1)}, u32[]{:S(2)}, u32[]{:S(2)}) collective-permute-start(f32[1,512]{1,0:T(1,128)S(1)} %get-tuple-element.159), channel_id=1, source_target_pairs={{1,0},{2,1},{3,2},{4,3},{5,4},{6,5},{7,6},{8,7},{9,8},{10,9},{11,1... | collective-permute-start | bytes 6152 | tf_op jit(solution)/shard_map/ppermute | solution.py:19
  19.2 11.5 %collective-permute-start.1 = (f32[1,512]{1,0:T(1,128)S(1)}, f32[1,512]{1,0:T(1,128)S(1)}, u32[]{:S(2)}, u32[]{:S(2)}) collective-permute-start(f32[1,512]{1,0:T(1,128)S(1)} %get-tuple-element.160), channel_id=1, source_target_pairs={{0,1},{1,2},{2,3},{3,4},{4,5},{5,6},{6,7},{7,8},{8,9},{9,10},{10,1... | collective-permute-start | bytes 6152 | tf_op jit(solution)/shard_map/ppermute | solution.py:17
  34.3 11.5 %collective-permute-start.3 = (f32[1,512]{1,0:T(1,128)S(1)}, f32[1,512]{1,0:T(1,128)S(1)}, u32[]{:S(2)}, u32[]{:S(2)}) collective-permute-start(f32[1,512]{1,0:T(1,128)S(1)} %get-tuple-element.158), channel_id=1, source_target_pairs={{0,1},{1,2},{2,3},{3,4},{4,5},{5,6},{6,7},{7,8},{8,9},{9,10},{10,1... | collective-permute-start | bytes 6152 | tf_op jit(solution)/shard_map/ppermute | solution.py:17
  49.4 11.5 %collective-permute-start.5 = (f32[1,512]{1,0:T(1,128)S(1)}, f32[1,512]{1,0:T(1,128)S(1)}, u32[]{:S(2)}, u32[]{:S(2)}) collective-permute-start(f32[1,512]{1,0:T(1,128)S(1)} %get-tuple-element.156), channel_id=1, source_target_pairs={{0,1},{1,2},{2,3},{3,4},{4,5},{5,6},{6,7},{7,8},{8,9},{9,10},{10,1... | collective-permute-start | bytes 6152 | tf_op jit(solution)/shard_map/ppermute | solution.py:17
  64.4 11.5 %collective-permute-start.7 = (f32[1,512]{1,0:T(1,128)S(1)}, f32[1,512]{1,0:T(1,128)S(1)}, u32[]{:S(2)}, u32[]{:S(2)}) collective-permute-start(f32[1,512]{1,0:T(1,128)S(1)} %get-tuple-element.154), channel_id=1, source_target_pairs={{0,1},{1,2},{2,3},{3,4},{4,5},{5,6},{6,7},{7,8},{8,9},{9,10},{10,1... | collective-permute-start | bytes 6152 | tf_op jit(solution)/shard_map/ppermute | solution.py:17
  79.6 11.5 %collective-permute-start.9 = (f32[1,512]{1,0:T(1,128)S(1)}, f32[1,512]{1,0:T(1,128)S(1)}, u32[]{:S(2)}, u32[]{:S(2)}) collective-permute-start(f32[1,512]{1,0:T(1,128)S(1)} %get-tuple-element.152), channel_id=1, source_target_pairs={{0,1},{1,2},{2,3},{3,4},{4,5},{5,6},{6,7},{7,8},{8,9},{9,10},{10,1... | collective-permute-start | bytes 6152 | tf_op jit(solution)/shard_map/ppermute | solution.py:17
  94.7 11.5 %collective-permute-start.11 = (f32[1,512]{1,0:T(1,128)S(1)}, f32[1,512]{1,0:T(1,128)S(1)}, u32[]{:S(2)}, u32[]{:S(2)}) collective-permute-start(f32[1,512]{1,0:T(1,128)S(1)} %get-tuple-element.150), channel_id=1, source_target_pairs={{0,1},{1,2},{2,3},{3,4},{4,5},{5,6},{6,7},{7,8},{8,9},{9,10},{10,1... | collective-permute-start | bytes 6152 | tf_op jit(solution)/shard_map/ppermute | solution.py:17
  109.7 11.5 %collective-permute-start.13 = (f32[1,512]{1,0:T(1,128)S(1)}, f32[1,512]{1,0:T(1,128)S(1)}, u32[]{:S(2)}, u32[]{:S(2)}) collective-permute-start(f32[1,512]{1,0:T(1,128)S(1)} %get-tuple-element.148), channel_id=1, source_target_pairs={{0,1},{1,2},{2,3},{3,4},{4,5},{5,6},{6,7},{7,8},{8,9},{9,10},{10,1... | collective-permute-start | bytes 6152 | tf_op jit(solution)/shard_map/ppermute | solution.py:17
  124.7 11.5 %collective-permute-start.15 = (f32[1,512]{1,0:T(1,128)S(1)}, f32[1,512]{1,0:T(1,128)S(1)}, u32[]{:S(2)}, u32[]{:S(2)}) collective-permute-start(f32[1,512]{1,0:T(1,128)S(1)} %get-tuple-element.146), channel_id=1, source_target_pairs={{0,1},{1,2},{2,3},{3,4},{4,5},{5,6},{6,7},{7,8},{8,9},{9,10},{10,1... | collective-permute-start | bytes 6152 | tf_op jit(solution)/shard_map/ppermute | solution.py:17
  145.7 11.5 %collective-permute-start.18 = (f32[1,512]{1,0:T(1,128)S(1)}, f32[1,512]{1,0:T(1,128)S(1)}, u32[]{:S(2)}, u32[]{:S(2)}) collective-permute-start(f32[1,512]{1,0:T(1,128)S(1)} %get-tuple-element.144), channel_id=1, source_target_pairs={{0,1},{1,2},{2,3},{3,4},{4,5},{5,6},{6,7},{7,8},{8,9},{9,10},{10,1... | collective-permute-start | bytes 6152 | tf_op jit(solution)/shard_map/ppermute | solution.py:17
  159.9 11.5 %collective-permute-start.20 = (f32[1,512]{1,0:T(1,128)S(1)}, f32[1,512]{1,0:T(1,128)S(1)}, u32[]{:S(2)}, u32[]{:S(2)}) collective-permute-start(f32[1,512]{1,0:T(1,128)S(1)} %get-tuple-element.142), channel_id=1, source_target_pairs={{0,1},{1,2},{2,3},{3,4},{4,5},{5,6},{6,7},{7,8},{8,9},{9,10},{10,1... | collective-permute-start | bytes 6152 | tf_op jit(solution)/shard_map/ppermute | solution.py:17
  174.2 11.5 %collective-permute-start.22 = (f32[1,512]{1,0:T(1,128)S(1)}, f32[1,512]{1,0:T(1,128)S(1)}, u32[]{:S(2)}, u32[]{:S(2)}) collective-permute-start(f32[1,512]{1,0:T(1,128)S(1)} %get-tuple-element.140), channel_id=1, source_target_pairs={{0,1},{1,2},{2,3},{3,4},{4,5},{5,6},{6,7},{7,8},{8,9},{9,10},{10,1... | collective-permute-start | bytes 6152 | tf_op jit(solution)/shard_map/ppermute | solution.py:17
  188.4 11.5 %collective-permute-start.24 = (f32[1,512]{1,0:T(1,128)S(1)}, f32[1,512]{1,0:T(1,128)S(1)}, u32[]{:S(2)}, u32[]{:S(2)}) collective-permute-start(f32[1,512]{1,0:T(1,128)S(1)} %get-tuple-element.138), channel_id=1, source_target_pairs={{0,1},{1,2},{2,3},{3,4},{4,5},{5,6},{6,7},{7,8},{8,9},{9,10},{10,1... | collective-permute-start | bytes 6152 | tf_op jit(solution)/shard_map/ppermute | solution.py:17
  245.3 11.6 %collective-permute-start.32 = (f32[1,512]{1,0:T(1,128)S(1)}, f32[1,512]{1,0:T(1,128)S(1)}, u32[]{:S(2)}, u32[]{:S(2)}) collective-permute-start(f32[1,512]{1,0:T(1,128)S(1)} %get-tuple-element.130), channel_id=1, source_target_pairs={{0,1},{1,2},{2,3},{3,4},{4,5},{5,6},{6,7},{7,8},{8,9},{9,10},{10,1... | collective-permute-start | bytes 6152 | tf_op jit(solution)/shard_map/ppermute | solution.py:17
  258.4 420.1 %all-gather.7.cloned.1.call-start = ((), (), s32[]{:S(2)}) async-start(), calls=%async_computation.1 | async-start | bytes 1622016 | tf_op jit(solution)/shard_map/all_gather | solution.py:74
  383.3 11.5 %collective-permute-start.35 = (f32[1,512]{1,0:T(1,128)S(1)}, f32[1,512]{1,0:T(1,128)S(1)}, u32[]{:S(2)}, u32[]{:S(2)}) collective-permute-start(f32[1,512]{1,0:T(1,128)S(1)} %get-tuple-element.128), channel_id=1, source_target_pairs={{0,1},{1,2},{2,3},{3,4},{4,5},{5,6},{6,7},{7,8},{8,9},{9,10},{10,1... | collective-permute-start | bytes 6152 | tf_op jit(solution)/shard_map/ppermute | solution.py:17
  473.5 11.5 %collective-permute-start.47 = (f32[1,512]{1,0:T(1,128)S(1)}, f32[1,512]{1,0:T(1,128)S(1)}, u32[]{:S(2)}, u32[]{:S(2)}) collective-permute-start(f32[1,512]{1,0:T(1,128)S(1)} %get-tuple-element.116), channel_id=1, source_target_pairs={{0,1},{1,2},{2,3},{3,4},{4,5},{5,6},{6,7},{7,8},{8,9},{9,10},{10,1... | collective-permute-start | bytes 6152 | tf_op jit(solution)/shard_map/ppermute | solution.py:17
  488.5 11.5 %collective-permute-start.49 = (f32[1,512]{1,0:T(1,128)S(1)}, f32[1,512]{1,0:T(1,128)S(1)}, u32[]{:S(2)}, u32[]{:S(2)}) collective-permute-start(f32[1,512]{1,0:T(1,128)S(1)} %get-tuple-element.114), channel_id=1, source_target_pairs={{0,1},{1,2},{2,3},{3,4},{4,5},{5,6},{6,7},{7,8},{8,9},{9,10},{10,1... | collective-permute-start | bytes 6152 | tf_op jit(solution)/shard_map/ppermute | solution.py:17
  552.2 11.5 %collective-permute-start.58 = (f32[1,512]{1,0:T(1,128)S(1)}, f32[1,512]{1,0:T(1,128)S(1)}, u32[]{:S(2)}, u32[]{:S(2)}) collective-permute-start(f32[1,512]{1,0:T(1,128)S(1)} %get-tuple-element.106), channel_id=1, source_target_pairs={{0,1},{1,2},{2,3},{3,4},{4,5},{5,6},{6,7},{7,8},{8,9},{9,10},{10,1... | collective-permute-start | bytes 6152 | tf_op jit(solution)/shard_map/ppermute | solution.py:17
  566.4 11.5 %collective-permute-start.60 = (f32[1,512]{1,0:T(1,128)S(1)}, f32[1,512]{1,0:T(1,128)S(1)}, u32[]{:S(2)}, u32[]{:S(2)}) collective-permute-start(f32[1,512]{1,0:T(1,128)S(1)} %get-tuple-element.104), channel_id=1, source_target_pairs={{0,1},{1,2},{2,3},{3,4},{4,5},{5,6},{6,7},{7,8},{8,9},{9,10},{10,1... | collective-permute-start | bytes 6152 | tf_op jit(solution)/shard_map/ppermute | solution.py:17
  580.6 11.5 %collective-permute-start.62 = (f32[1,512]{1,0:T(1,128)S(1)}, f32[1,512]{1,0:T(1,128)S(1)}, u32[]{:S(2)}, u32[]{:S(2)}) collective-permute-start(f32[1,512]{1,0:T(1,128)S(1)} %get-tuple-element.102), channel_id=1, source_target_pairs={{0,1},{1,2},{2,3},{3,4},{4,5},{5,6},{6,7},{7,8},{8,9},{9,10},{10,1... | collective-permute-start | bytes 6152 | tf_op jit(solution)/shard_map/ppermute | solution.py:17
  609.1 11.5 %collective-permute-start.66 = (f32[1,512]{1,0:T(1,128)S(1)}, f32[1,512]{1,0:T(1,128)S(1)}, u32[]{:S(2)}, u32[]{:S(2)}) collective-permute-start(f32[1,512]{1,0:T(1,128)S(1)} %get-tuple-element.98), channel_id=1, source_target_pairs={{0,1},{1,2},{2,3},{3,4},{4,5},{5,6},{6,7},{7,8},{8,9},{9,10},{10,1... | collective-permute-start | bytes 6152 | tf_op jit(solution)/shard_map/ppermute | solution.py:17
  776.5 11.5 %collective-permute-start.73 = (f32[1,512]{1,0:T(1,128)S(1)}, f32[1,512]{1,0:T(1,128)S(1)}, u32[]{:S(2)}, u32[]{:S(2)}) collective-permute-start(f32[1,512]{1,0:T(1,128)S(1)} %get-tuple-element.92), channel_id=1, source_target_pairs={{0,1},{1,2},{2,3},{3,4},{4,5},{5,6},{6,7},{7,8},{8,9},{9,10},{10,1... | collective-permute-start | bytes 6152 | tf_op jit(solution)/shard_map/ppermute | solution.py:17
  (67 other events, 846.9 us)
Sparse Core Ops, SparseCore 0:
  258.5 55.1 all-gather.4
  622.1 56.3 all-gather.6
where the time goes:
time: 859 us; the launch traced here: 854 us
  waiting for transfers between devices  424 us (49%)
  starting transfers between devices  259 us (30%)
  matrix products  142 us (17%)
  between operations  15.1 us (2%)
    ppermute x39, waiting for transfers between devices, with_halo(): lax.ppermute(tail, axis, [(i, (i + 1) % count) for i in range(count)])  300 us
    ppermute x39, starting transfers between devices, with_halo(): lax.ppermute(tail, axis, [(i, (i + 1) % count) for i in range(count)])  147 us
    dot_general x99, matrix products, apply_matrix(): jnp.dot(field, matrix, precision=HIGHEST, preferred_element_type=jnp.floa...  142 us
    all_gather x2, waiting for transfers between devices, per_device(): lax.all_gather(residual[None].astype(jnp.bfloat16), 'tm', axis=0, tiled=T...  112 us
    ppermute x39, starting transfers between devices, with_halo(): lax.ppermute(head, axis, [((i + 1) % count, i) for i in range(count)])  100 us
  transfers between devices with their start and end apart: 84, of which 45 were waited for; matrix products, arithmetic and copies ran while one was open for 0% of the time, Pallas kernels for 0%

commit v1 on v0

--- a/solution.py
+++ b/solution.py
@@ -71,8 +71,11 @@
             begin_state = previous(end_values)
         end_values = relax_block(begin_state, block_steps)[-1]
         residual = relax_block(previous(end_values), block_steps)[-1] - end_values
-        gathered = lax.all_gather(
-            residual[None].astype(jnp.bfloat16), "tm", axis=0, tiled=True
+        gathered = jnp.concatenate(
+            lax.all_to_all(
+                jnp.stack([residual[None].astype(jnp.bfloat16)] * lax.axis_size("tm")), "tm", 0, 0
+            ),
+            axis=0,
         ).astype(jnp.float32)
 
         def coarse_turn(source, carried):

time: 859 us -> 806 us (0.938)
  waiting for transfers between devices: 424 us -> 380 us
  between operations: 15.1 us -> 1.73 us
    all_gather x2 -> x0, waiting for transfers between devices: 112 us -> none  [per_device(): lax.all_gather(residual[None].astype(jnp.bfloat16), 'tm', axis=0, tiled=T...]
    all_to_all x0 -> x2, waiting for transfers between devices: none -> 70.7 us  [per_device(): lax.all_to_all(jnp.stack([residual[None].astype(jnp.bfloat16)] * lax.axis...]
    all_to_all x0 -> x2, starting transfers between devices: none -> 15.3 us  [per_device(): lax.all_to_all(jnp.stack([residual[None].astype(jnp.bfloat16)] * lax.axis...]
    ppermute x39, starting transfers between devices: 100 us -> 85.9 us  [with_halo(): lax.ppermute(head, axis, [((i + 1) % count, i) for i in range(count)])]
where the time goes in v1:
time: 806 us; the launch traced here: 801 us
  waiting for transfers between devices  380 us (47%)
  starting transfers between devices  264 us (33%)
  matrix products  141 us (17%)
    ppermute x39, waiting for transfers between devices, with_halo(): lax.ppermute(tail, axis, [(i, (i + 1) % count) for i in range(count)])  297 us
    ppermute x39, starting transfers between devices, with_halo(): lax.ppermute(tail, axis, [(i, (i + 1) % count) for i in range(count)])  151 us
    dot_general x99, matrix products, apply_matrix(): jnp.dot(field, matrix, precision=HIGHEST, preferred_element_type=jnp.floa...  141 us
    ppermute x39, starting transfers between devices, with_halo(): lax.ppermute(head, axis, [((i + 1) % count, i) for i in range(count)])  85.9 us
    all_to_all x2, waiting for transfers between devices, per_device(): lax.all_to_all(jnp.stack([residual[None].astype(jnp.bfloat16)] * lax.axis...  70.7 us
  transfers between devices with their start and end apart: 84, of which 45 were waited for; matrix products, arithmetic and copies ran while one was open for 0% of the time, Pallas kernels for 0%

profile of v1, /device:TPU:102, one launch (start us, length us, event | category | flops | bytes accessed | tf_op | source)
XLA Modules:
  0.0 800.7 jit_solution(7189558526312150200)
XLA Ops:
  0.1 12.6 %collective-permute-start = (f32[1,512]{1,0:T(1,128)S(1)}, f32[1,512]{1,0:T(1,128)S(1)}, u32[]{:S(2)}, u32[]{:S(2)}) collective-permute-start(f32[1,512]{1,0:T(1,128)S(1)} %get-tuple-element.163), channel_id=1, source_target_pairs={{1,0},{2,1},{3,2},{4,3},{5,4},{6,5},{7,6},{8,7},{9,8},{10,9},{11,1... | collective-permute-start | bytes 6152 | tf_op jit(solution)/shard_map/ppermute | solution.py:19
  14.6 9.6 %collective-permute-done.1 = f32[1,512]{1,0:T(1,128)S(1)} collective-permute-done((f32[1,512]{1,0:T(1,128)S(1)}, f32[1,512]{1,0:T(1,128)S(1)}, u32[]{:S(2)}, u32[]{:S(2)}) %collective-permute-start.1) | collective-permute-done | bytes 2080 | tf_op jit(solution)/shard_map/ppermute | solution.py:17
  31.7 7.6 collective-permute-done.3
  46.8 7.6 collective-permute-done.5
  61.9 7.6 collective-permute-done.7
  77.0 7.6 collective-permute-done.9
  92.1 7.6 collective-permute-done.11
  107.1 7.6 collective-permute-done.13
  122.1 7.6 collective-permute-done.15
  143.1 7.6 collective-permute-done.18
  157.3 7.6 collective-permute-done.20
  171.6 7.6 collective-permute-done.22
  185.8 7.6 collective-permute-done.24
  200.0 7.6 collective-permute-done.26
  214.3 7.6 collective-permute-done.28
  228.5 7.6 collective-permute-done.30
  252.6 7.8 all-to-all-start
  260.4 35.4 %all-to-all-done = bf16[32,1,48,512]{3,2,1,0:T(8,128)(2,1)} async-done(((bf16[32,1,48,512]{3,2,1,0:T(8,128)(2,1)}), bf16[32,1,48,512]{3,2,1,0:T(8,128)(2,1)}, u32[]{:S(2)}, u32[]{:S(2)}) %all-to-all-start) | async-done | bytes 1572896 | tf_op jit(solution)/shard_map/all_to_all | solution.py:75
  299.3 50.1 %while.20 = (s32[]{:T(128)}, f32[48,512]{1,0:T(8,128)S(1)}, s32[]{:T(128)}, f32[512,512]{1,0:T(8,128)S(1)}, f32[32,48,512]{2,1,0:T(8,128)}, /*index=5*/s32[]{:T(128)}, s32[]{:T(128)}, s32[]{:T(128)}) while((s32[]{:T(128)}, f32[48,512]{1,0:T(8,128)S(1)}, s32[]{:T(128)}, f32[512,512]{1,0:T(8,128)S(1)}, f32[32,48,512]{2,1,0:T(8,128)}, ...), condition=%wide.region_1.2_spmd, body=%wide.region_0.1_spmd.sunk | while | flops 151019520 | bytes 1540219 | solution.py:84
  487.5 7.6 collective-permute-done.52
  573.1 7.6 collective-permute-done.64
  604.5 35.4 %all-to-all-done.1 = bf16[32,1,48,512]{3,2,1,0:T(8,128)(2,1)} async-done(((bf16[32,1,48,512]{3,2,1,0:T(8,128)(2,1)}), bf16[32,1,48,512]{3,2,1,0:T(8,128)(2,1)}, u32[]{:S(2)}, u32[]{:S(2)}) %all-to-all-start.1) | async-done | bytes 1572896 | tf_op jit(solution)/shard_map/all_to_all | solution.py:75
  643.5 50.1 %while.21 = (s32[]{:T(128)}, f32[48,512]{1,0:T(8,128)S(1)}, s32[]{:T(128)}, f32[512,512]{1,0:T(8,128)S(1)}, f32[32,48,512]{2,1,0:T(8,128)}, /*index=5*/s32[]{:T(128)}, s32[]{:T(128)}, s32[]{:T(128)}) while((s32[]{:T(128)}, f32[48,512]{1,0:T(8,128)S(1)}, s32[]{:T(128)}, f32[512,512]{1,0:T(8,128)S(1)}, f32[32,48,512]{2,1,0:T(8,128)}, ...), condition=%wide.region_3.4_spmd, body=%wide.region_2.3_spmd.sunk | while | flops 151019520 | bytes 1540219 | solution.py:84
  790.8 7.6 collective-permute-done.81
  (372 shorter events, 567.5 us)
Async XLA Ops:
  0.1 14.6 %collective-permute-start = (f32[1,512]{1,0:T(1,128)S(1)}, f32[1,512]{1,0:T(1,128)S(1)}, u32[]{:S(2)}, u32[]{:S(2)}) collective-permute-start(f32[1,512]{1,0:T(1,128)S(1)} %get-tuple-element.163), channel_id=1, source_target_pairs={{1,0},{2,1},{3,2},{4,3},{5,4},{6,5},{7,6},{8,7},{9,8},{10,9},{11,1... | collective-permute-start | bytes 6152 | tf_op jit(solution)/shard_map/ppermute | solution.py:19
  12.7 11.5 %collective-permute-start.1 = (f32[1,512]{1,0:T(1,128)S(1)}, f32[1,512]{1,0:T(1,128)S(1)}, u32[]{:S(2)}, u32[]{:S(2)}) collective-permute-start(f32[1,512]{1,0:T(1,128)S(1)} %get-tuple-element.164), channel_id=1, source_target_pairs={{0,1},{1,2},{2,3},{3,4},{4,5},{5,6},{6,7},{7,8},{8,9},{9,10},{10,1... | collective-permute-start | bytes 6152 | tf_op jit(solution)/shard_map/ppermute | solution.py:17
  42.8 11.5 %collective-permute-start.5 = (f32[1,512]{1,0:T(1,128)S(1)}, f32[1,512]{1,0:T(1,128)S(1)}, u32[]{:S(2)}, u32[]{:S(2)}) collective-permute-start(f32[1,512]{1,0:T(1,128)S(1)} %get-tuple-element.160), channel_id=1, source_target_pairs={{0,1},{1,2},{2,3},{3,4},{4,5},{5,6},{6,7},{7,8},{8,9},{9,10},{10,1... | collective-permute-start | bytes 6152 | tf_op jit(solution)/shard_map/ppermute | solution.py:17
  57.9 11.5 %collective-permute-start.7 = (f32[1,512]{1,0:T(1,128)S(1)}, f32[1,512]{1,0:T(1,128)S(1)}, u32[]{:S(2)}, u32[]{:S(2)}) collective-permute-start(f32[1,512]{1,0:T(1,128)S(1)} %get-tuple-element.158), channel_id=1, source_target_pairs={{0,1},{1,2},{2,3},{3,4},{4,5},{5,6},{6,7},{7,8},{8,9},{9,10},{10,1... | collective-permute-start | bytes 6152 | tf_op jit(solution)/shard_map/ppermute | solution.py:17
  73.1 11.5 %collective-permute-start.9 = (f32[1,512]{1,0:T(1,128)S(1)}, f32[1,512]{1,0:T(1,128)S(1)}, u32[]{:S(2)}, u32[]{:S(2)}) collective-permute-start(f32[1,512]{1,0:T(1,128)S(1)} %get-tuple-element.156), channel_id=1, source_target_pairs={{0,1},{1,2},{2,3},{3,4},{4,5},{5,6},{6,7},{7,8},{8,9},{9,10},{10,1... | collective-permute-start | bytes 6152 | tf_op jit(solution)/shard_map/ppermute | solution.py:17
  88.1 11.5 %collective-permute-start.11 = (f32[1,512]{1,0:T(1,128)S(1)}, f32[1,512]{1,0:T(1,128)S(1)}, u32[]{:S(2)}, u32[]{:S(2)}) collective-permute-start(f32[1,512]{1,0:T(1,128)S(1)} %get-tuple-element.154), channel_id=1, source_target_pairs={{0,1},{1,2},{2,3},{3,4},{4,5},{5,6},{6,7},{7,8},{8,9},{9,10},{10,1... | collective-permute-start | bytes 6152 | tf_op jit(solution)/shard_map/ppermute | solution.py:17
  103.2 11.5 %collective-permute-start.13 = (f32[1,512]{1,0:T(1,128)S(1)}, f32[1,512]{1,0:T(1,128)S(1)}, u32[]{:S(2)}, u32[]{:S(2)}) collective-permute-start(f32[1,512]{1,0:T(1,128)S(1)} %get-tuple-element.152), channel_id=1, source_target_pairs={{0,1},{1,2},{2,3},{3,4},{4,5},{5,6},{6,7},{7,8},{8,9},{9,10},{10,1... | collective-permute-start | bytes 6152 | tf_op jit(solution)/shard_map/ppermute | solution.py:17
  139.2 11.5 %collective-permute-start.18 = (f32[1,512]{1,0:T(1,128)S(1)}, f32[1,512]{1,0:T(1,128)S(1)}, u32[]{:S(2)}, u32[]{:S(2)}) collective-permute-start(f32[1,512]{1,0:T(1,128)S(1)} %get-tuple-element.148), channel_id=1, source_target_pairs={{0,1},{1,2},{2,3},{3,4},{4,5},{5,6},{6,7},{7,8},{8,9},{9,10},{10,1... | collective-permute-start | bytes 6152 | tf_op jit(solution)/shard_map/ppermute | solution.py:17
  153.4 11.5 %collective-permute-start.20 = (f32[1,512]{1,0:T(1,128)S(1)}, f32[1,512]{1,0:T(1,128)S(1)}, u32[]{:S(2)}, u32[]{:S(2)}) collective-permute-start(f32[1,512]{1,0:T(1,128)S(1)} %get-tuple-element.146), channel_id=1, source_target_pairs={{0,1},{1,2},{2,3},{3,4},{4,5},{5,6},{6,7},{7,8},{8,9},{9,10},{10,1... | collective-permute-start | bytes 6152 | tf_op jit(solution)/shard_map/ppermute | solution.py:17
  167.6 11.5 %collective-permute-start.22 = (f32[1,512]{1,0:T(1,128)S(1)}, f32[1,512]{1,0:T(1,128)S(1)}, u32[]{:S(2)}, u32[]{:S(2)}) collective-permute-start(f32[1,512]{1,0:T(1,128)S(1)} %get-tuple-element.144), channel_id=1, source_target_pairs={{0,1},{1,2},{2,3},{3,4},{4,5},{5,6},{6,7},{7,8},{8,9},{9,10},{10,1... | collective-permute-start | bytes 6152 | tf_op jit(solution)/shard_map/ppermute | solution.py:17
  210.3 11.5 %collective-permute-start.28 = (f32[1,512]{1,0:T(1,128)S(1)}, f32[1,512]{1,0:T(1,128)S(1)}, u32[]{:S(2)}, u32[]{:S(2)}) collective-permute-start(f32[1,512]{1,0:T(1,128)S(1)} %get-tuple-element.138), channel_id=1, source_target_pairs={{0,1},{1,2},{2,3},{3,4},{4,5},{5,6},{6,7},{7,8},{8,9},{9,10},{10,1... | collective-permute-start | bytes 6152 | tf_op jit(solution)/shard_map/ppermute | solution.py:17
  252.6 43.1 %all-to-all-start = ((bf16[32,1,48,512]{3,2,1,0:T(8,128)(2,1)}), bf16[32,1,48,512]{3,2,1,0:T(8,128)(2,1)}, u32[]{:S(2)}, u32[]{:S(2)}) async-start(bf16[32,1,48,512]{3,2,1,0:T(8,128)(2,1)} %stack.22), calls=%async_computation | async-start | bytes 3145728 | tf_op jit(solution)/shard_map/all_to_all | solution.py:75
  387.4 11.5 %collective-permute-start.39 = (f32[1,512]{1,0:T(1,128)S(1)}, f32[1,512]{1,0:T(1,128)S(1)}, u32[]{:S(2)}, u32[]{:S(2)}) collective-permute-start(f32[1,512]{1,0:T(1,128)S(1)} %get-tuple-element.128), channel_id=1, source_target_pairs={{0,1},{1,2},{2,3},{3,4},{4,5},{5,6},{6,7},{7,8},{8,9},{9,10},{10,1... | collective-permute-start | bytes 6152 | tf_op jit(solution)/shard_map/ppermute | solution.py:17
  432.5 11.5 %collective-permute-start.45 = (f32[1,512]{1,0:T(1,128)S(1)}, f32[1,512]{1,0:T(1,128)S(1)}, u32[]{:S(2)}, u32[]{:S(2)}) collective-permute-start(f32[1,512]{1,0:T(1,128)S(1)} %get-tuple-element.122), channel_id=1, source_target_pairs={{0,1},{1,2},{2,3},{3,4},{4,5},{5,6},{6,7},{7,8},{8,9},{9,10},{10,1... | collective-permute-start | bytes 6152 | tf_op jit(solution)/shard_map/ppermute | solution.py:17
  462.6 11.5 %collective-permute-start.49 = (f32[1,512]{1,0:T(1,128)S(1)}, f32[1,512]{1,0:T(1,128)S(1)}, u32[]{:S(2)}, u32[]{:S(2)}) collective-permute-start(f32[1,512]{1,0:T(1,128)S(1)} %get-tuple-element.118), channel_id=1, source_target_pairs={{0,1},{1,2},{2,3},{3,4},{4,5},{5,6},{6,7},{7,8},{8,9},{9,10},{10,1... | collective-permute-start | bytes 6152 | tf_op jit(solution)/shard_map/ppermute | solution.py:17
  483.6 11.5 %collective-permute-start.52 = (f32[1,512]{1,0:T(1,128)S(1)}, f32[1,512]{1,0:T(1,128)S(1)}, u32[]{:S(2)}, u32[]{:S(2)}) collective-permute-start(f32[1,512]{1,0:T(1,128)S(1)} %get-tuple-element.116), channel_id=1, source_target_pairs={{0,1},{1,2},{2,3},{3,4},{4,5},{5,6},{6,7},{7,8},{8,9},{9,10},{10,1... | collective-permute-start | bytes 6152 | tf_op jit(solution)/shard_map/ppermute | solution.py:17
  497.8 11.5 %collective-permute-start.54 = (f32[1,512]{1,0:T(1,128)S(1)}, f32[1,512]{1,0:T(1,128)S(1)}, u32[]{:S(2)}, u32[]{:S(2)}) collective-permute-start(f32[1,512]{1,0:T(1,128)S(1)} %get-tuple-element.114), channel_id=1, source_target_pairs={{0,1},{1,2},{2,3},{3,4},{4,5},{5,6},{6,7},{7,8},{8,9},{9,10},{10,1... | collective-permute-start | bytes 6152 | tf_op jit(solution)/shard_map/ppermute | solution.py:17
  540.5 11.7 %collective-permute-start.60 = (f32[1,512]{1,0:T(1,128)S(1)}, f32[1,512]{1,0:T(1,128)S(1)}, u32[]{:S(2)}, u32[]{:S(2)}) collective-permute-start(f32[1,512]{1,0:T(1,128)S(1)} %get-tuple-element.108), channel_id=1, source_target_pairs={{0,1},{1,2},{2,3},{3,4},{4,5},{5,6},{6,7},{7,8},{8,9},{9,10},{10,1... | collective-permute-start | bytes 6152 | tf_op jit(solution)/shard_map/ppermute | solution.py:17
  569.1 11.5 %collective-permute-start.64 = (f32[1,512]{1,0:T(1,128)S(1)}, f32[1,512]{1,0:T(1,128)S(1)}, u32[]{:S(2)}, u32[]{:S(2)}) collective-permute-start(f32[1,512]{1,0:T(1,128)S(1)} %get-tuple-element.104), channel_id=1, source_target_pairs={{0,1},{1,2},{2,3},{3,4},{4,5},{5,6},{6,7},{7,8},{8,9},{9,10},{10,1... | collective-permute-start | bytes 6152 | tf_op jit(solution)/shard_map/ppermute | solution.py:17
  583.4 11.5 %collective-permute-start.66 = (f32[1,512]{1,0:T(1,128)S(1)}, f32[1,512]{1,0:T(1,128)S(1)}, u32[]{:S(2)}, u32[]{:S(2)}) collective-permute-start(f32[1,512]{1,0:T(1,128)S(1)} %get-tuple-element.102), channel_id=1, source_target_pairs={{0,1},{1,2},{2,3},{3,4},{4,5},{5,6},{6,7},{7,8},{8,9},{9,10},{10,1... | collective-permute-start | bytes 6152 | tf_op jit(solution)/shard_map/ppermute | solution.py:17
  597.0 42.9 %all-to-all-start.1 = ((bf16[32,1,48,512]{3,2,1,0:T(8,128)(2,1)}), bf16[32,1,48,512]{3,2,1,0:T(8,128)(2,1)}, u32[]{:S(2)}, u32[]{:S(2)}) async-start(bf16[32,1,48,512]{3,2,1,0:T(8,128)(2,1)} %stack.23), calls=%async_computation.1 | async-start | bytes 3145728 | tf_op jit(solution)/shard_map/all_to_all | solution.py:75
  715.7 11.5 %collective-permute-start.71 = (f32[1,512]{1,0:T(1,128)S(1)}, f32[1,512]{1,0:T(1,128)S(1)}, u32[]{:S(2)}, u32[]{:S(2)}) collective-permute-start(f32[1,512]{1,0:T(1,128)S(1)} %get-tuple-element.98), channel_id=1, source_target_pairs={{0,1},{1,2},{2,3},{3,4},{4,5},{5,6},{6,7},{7,8},{8,9},{9,10},{10,1... | collective-permute-start | bytes 6152 | tf_op jit(solution)/shard_map/ppermute | solution.py:17
  744.2 11.5 %collective-permute-start.75 = (f32[1,512]{1,0:T(1,128)S(1)}, f32[1,512]{1,0:T(1,128)S(1)}, u32[]{:S(2)}, u32[]{:S(2)}) collective-permute-start(f32[1,512]{1,0:T(1,128)S(1)} %get-tuple-element.94), channel_id=1, source_target_pairs={{0,1},{1,2},{2,3},{3,4},{4,5},{5,6},{6,7},{7,8},{8,9},{9,10},{10,1... | collective-permute-start | bytes 6152 | tf_op jit(solution)/shard_map/ppermute | solution.py:17
  786.9 11.5 %collective-permute-start.81 = (f32[1,512]{1,0:T(1,128)S(1)}, f32[1,512]{1,0:T(1,128)S(1)}, u32[]{:S(2)}, u32[]{:S(2)}) collective-permute-start(f32[1,512]{1,0:T(1,128)S(1)} %get-tuple-element.88), channel_id=1, source_target_pairs={{0,1},{1,2},{2,3},{3,4},{4,5},{5,6},{6,7},{7,8},{8,9},{9,10},{10,1... | collective-permute-start | bytes 6152 | tf_op jit(solution)/shard_map/ppermute | solution.py:17
  (67 other events, 802.6 us)
